TPU v7x, 32 devices: a whole 2x2x4 slice. The times are simulated.
32 devices in a mesh: grp: 4 (over z), tp: 8 (over y, x, core).
Axes of the slice: x: 2, y: 2, z: 4, core: 2. Of those that a mesh axis runs over, the one named last changes fastest.
Arguments:
- hidden: bfloat16 [1024, 8192], P('grp'), may hold values from -30 to 30
- proj_weight: bfloat16 [8192, 8192], P(None, 'tp'), may hold values from -0.32040776 to 0.32040776
- proj_bias: float32 [8192], P('tp'), may hold values from -3 to 3
- tile_pos: int32 [128], replicated, may hold values from 0 to 383, as said below
- text_embed: bfloat16 [3072, 8192], P('grp', 'tp'), may hold values from -76 to 76
- norm_gain: float32 [8192], P('tp'), may hold values from 0.25 to 1.75
- d_normed: bfloat16 [3072, 8192], P('grp', 'tp'), may hold values from -6 to 6
Outputs:
- normed: bfloat16 [3072, 8192], P('grp', 'tp')
- d_text: bfloat16 [3072, 8192], P('grp', 'tp')
- d_hidden: bfloat16 [1024, 8192], P('grp', 'tp')
Inputs may be any that keep to these rules, and one draw needn't show every extreme that they name: `tile_pos`: all positions are distinct. Of the tiles k * 32 to (k + 1) * 32 - 1, at most 8 lie in the 96 tile positions of one index of grp, and in every draw each such block has exactly 8 tiles in some index of grp.
All inputs are finite; a program needn't handle non-finite values.
Results may differ from a plain program's by a relative error of at most 0.015.
Values may be sent and summed in bfloat16 or wider, within the bound.
A program may use at most 64 MiB of HBM per device.

v0:
```python
import jax
import jax.numpy as jnp
from jax import lax
from jax.sharding import PartitionSpec as P

TILE = 8


epsilon = 1e-05


def gelu_slope(values):
    normal_cdf = 0.5 * (1.0 + lax.erf(values * 0.7071067811865476))
    density = jnp.exp(-0.5 * values * values) * 0.3989422804014327
    return normal_cdf + values * density


def match_table(wanted, choices_count):
    return wanted[None, :] == jnp.arange(choices_count, dtype=jnp.int32)[:, None]


def on_device(hidden, proj_weight, proj_bias, tile_pos, text_embed, norm_gain, d_normed):
    rows_dev = hidden.shape[0]
    model_width = hidden.shape[1]
    local_cols = proj_weight.shape[1]
    tok_dev = text_embed.shape[0]
    groups = lax.axis_size("grp")
    group_index = lax.axis_index("grp")
    lane_index = lax.axis_index("tp")
    tiles_dev = rows_dev // TILE
    spread = tok_dev // TILE
    total_tiles = tiles_dev * groups
    tile_width = TILE * local_cols
    capacity = max(2, (tiles_dev + groups - 1) // groups)
    activated = jax.nn.gelu(hidden.astype(jnp.float32), approximate=False).astype(jnp.bfloat16)
    image_rows = jnp.dot(activated, proj_weight, preferred_element_type=jnp.float32) + proj_bias
    tile_rows = image_rows.astype(jnp.bfloat16).reshape(tiles_dev, tile_width)
    target = tile_pos // spread
    local_pos = tile_pos - group_index * spread
    hits = match_table(local_pos, spread)
    is_image = jnp.any(hits, axis=1)
    place = hits.astype(jnp.bfloat16)
    tile_index = jnp.arange(total_tiles, dtype=jnp.int32)
    source = tile_index // tiles_dev
    earlier = (
        (source[:, None] == source[None, :])
        & (target[:, None] == target[None, :])
        & (tile_index[None, :] < tile_index[:, None])
    )
    standing = jnp.sum(earlier.astype(jnp.int32), axis=1)
    send_slot = lax.dynamic_slice_in_dim(
        target * capacity + standing, group_index * tiles_dev, tiles_dev, 0
    )
    sender = match_table(send_slot, groups * capacity).astype(jnp.bfloat16)
    outgoing = jnp.dot(sender, tile_rows, preferred_element_type=jnp.float32).astype(jnp.bfloat16)
    incoming = lax.all_to_all(outgoing, "grp", split_axis=0, concat_axis=0, tiled=True)
    arrival = match_table(source * capacity + standing, groups * capacity).astype(jnp.bfloat16)
    receiver = lax.dot_general(
        place, arrival, (((1,), (1,)), ((), ())), preferred_element_type=jnp.float32
    ).astype(jnp.bfloat16)
    placed = jnp.dot(receiver, incoming, preferred_element_type=jnp.float32)
    base_rows = text_embed.reshape(spread, tile_width)
    merged = jnp.where(is_image[:, None], placed.astype(jnp.bfloat16), base_rows).reshape(
        tok_dev, local_cols
    )
    wide_merged = merged.astype(jnp.float32)
    grad_in = d_normed.astype(jnp.float32) * norm_gain
    squares, crosses = lax.psum(
        (jnp.sum(wide_merged * wide_merged, axis=1), jnp.sum(grad_in * wide_merged, axis=1)), "tp"
    )
    inverse = lax.rsqrt(squares / model_width + epsilon)[:, None]
    cross_mean = (crosses / model_width)[:, None]
    normed = (wide_merged * inverse * norm_gain).astype(jnp.bfloat16)
    d_merged = inverse * (grad_in - wide_merged * inverse * inverse * cross_mean)
    d_tiles = d_merged.reshape(spread, tile_width)
    d_text = (
        jnp.where(is_image[:, None], 0.0, d_tiles).astype(jnp.bfloat16).reshape(tok_dev, local_cols)
    )
    d_image_tiles = d_tiles.astype(jnp.bfloat16)
    back_out = lax.dot_general(
        receiver, d_image_tiles, (((0,), (0,)), ((), ())), preferred_element_type=jnp.float32
    ).astype(jnp.bfloat16)
    back_in = lax.all_to_all(back_out, "grp", split_axis=0, concat_axis=0, tiled=True)
    returned = lax.dot_general(
        sender, back_in, (((0,), (0,)), ((), ())), preferred_element_type=jnp.float32
    )
    d_image = returned.astype(jnp.bfloat16).reshape(rows_dev, local_cols)
    partial_grads = lax.dot_general(
        d_image, proj_weight, (((1,), (1,)), ((), ())), preferred_element_type=jnp.float32
    )
    d_act = lax.psum_scatter(
        partial_grads.astype(jnp.bfloat16), "tp", scatter_dimension=1, tiled=True
    ).astype(jnp.float32)
    own_hidden = lax.dynamic_slice_in_dim(hidden, lane_index * local_cols, local_cols, 1).astype(
        jnp.float32
    )
    d_hidden = (d_act * gelu_slope(own_hidden)).astype(jnp.bfloat16)
    return (normed, d_text, d_hidden)


def solution(mesh):
    in_specs = (
        P("grp", None),
        P(None, "tp"),
        P("tp"),
        P(),
        P("grp", "tp"),
        P("tp"),
        P("grp", "tp"),
    )
    out_specs = (P("grp", "tp"), P("grp", "tp"), P("grp", "tp"))
    return jax.shard_map(
        on_device, mesh=mesh, in_specs=in_specs, out_specs=out_specs, check_vma=False
    )
```

profile of v0, /device:TPU:0, one launch (start us, length us, event | category | flops | bytes accessed | tf_op | source)
XLA Modules:
  0.0 167.0 jit_solution(1093481023617490761)
XLA Ops:
  7.2 0.7 and_select_fusion
  7.8 0.2 convert_reduce_fusion
  8.0 24.0 %fusion.70 = bf16[256,1024]{1,0:T(8,128)(2,1)S(1)} fusion(bf16[8192,1024]{1,0:T(8,128)(2,1)} %param.8, bf16[256,8192]{1,0:T(8,128)(2,1)} %param.7, f32[1024]{0:T(1024)} %param.9), kind=kOutput, calls=%fused_computation.85 | convolution fusion | flops 4433903616 | bytes 21499904 | tf_op jit(solution)/shard_map/dot_general | solution.py:36
  32.1 0.2 reshape.67
  32.3 0.1 dynamic_slice.6
  32.4 0.0 copy-start
  32.4 1.1 fusion.2
  33.5 6.3 %all-to-all-start = ((bf16[4,8,8192]{2,1,0:T(8,128)(2,1)}), bf16[4,8,8192]{2,1,0:T(8,128)(2,1)S(1)}, u32[]{:S(2)}, u32[]{:S(2)}) async-start(bf16[4,8,8192]{2,1,0:T(8,128)(2,1)} %fusion.2), calls=%async_computation | async-start | bytes 1048576 | tf_op jit(solution)/shard_map/all_to_all | solution.py:56
  39.8 0.0 reduce-scatter.2.cloned.1.call-start
  39.8 0.1 fusion.84
  39.9 0.1 broadcast_in_dim.21
  40.0 0.1 broadcast_in_dim.22
  40.1 2.6 %reshape.68 = bf16[96,8192]{1,0:T(8,128)(2,1)S(1)} reshape(bf16[768,1024]{1,0:T(8,128)(2,1)} %param.11) | data formatting | bytes 3145728 | tf_op jit(solution)/shard_map/reshape | solution.py:62
  42.7 0.1 convolution_convert_fusion.5
  42.8 11.5 %all-to-all-done = bf16[4,8,8192]{2,1,0:T(8,128)(2,1)S(1)} async-done(((bf16[4,8,8192]{2,1,0:T(8,128)(2,1)}), bf16[4,8,8192]{2,1,0:T(8,128)(2,1)S(1)}, u32[]{:S(2)}, u32[]{:S(2)}) %all-to-all-start) | async-done | bytes 524320 | tf_op jit(solution)/shard_map/all_to_all | solution.py:56
  54.3 2.3 %fusion.1 = f32[96,8192]{1,0:T(8,128)} fusion(bf16[96,8192]{1,0:T(8,128)(2,1)S(1)} %reshape.68, bf16[96,32]{0,1:T(8,128)(2,1)S(1)} %convolution_convert_fusion.5, pred[96]{0:T(512)(128)(4,1)S(1)} %fusion.84, bf16[4,8,8192]{2,1,0:T(8,128)(2,1)S(1)} %all-to-all-done), kind=kOutput, calls=%fused_computation.6 | convolution fusion | flops 52690944 | bytes 5249120 | tf_op jit(solution)/shard_map/dot_general | solution.py:61
  56.6 2.9 %reshape.70 = f32[768,1024]{1,0:T(8,128)S(1)} reshape(f32[96,8192]{1,0:T(8,128)} %fusion.1) | data formatting | bytes 6291456 | tf_op jit(solution)/shard_map/convert_element_type | solution.py:66
  59.4 0.0 copy-done
  59.5 2.1 %multiply_reduce_fusion = (f32[768]{0:T(1024)S(1)}, f32[768]{0:T(1024)S(1)}) fusion(f32[768,1024]{1,0:T(8,128)S(1)} %reshape.70, bf16[768,1024]{1,0:T(8,128)(2,1)} %param.13, f32[1024]{0:T(1024)S(1)} %copy-done), kind=kLoop, calls=%fused_computation.76 | loop fusion | flops 4717056 | bytes 4728832 | tf_op jit(solution)/shard_map/reduce_sum | solution.py:69
  61.6 13.1 %all-reduce = (f32[768]{0:T(1024)S(1)}, f32[768]{0:T(1024)S(1)}) all-reduce(f32[768]{0:T(1024)S(1)} %get-tuple-element.4, f32[768]{0:T(1024)S(1)} %get-tuple-element.3), channel_id=1, replica_groups=mesh['grp'=4,'tp'=8] {'tp'}, use_global_device_ids=true, to_apply=%region_3.4 | all-reduce | flops 1536 | bytes 12288 | tf_op jit(solution)/shard_map/psum | solution.py:68
  74.7 4.0 %fusion.119 = (bf16[768,1024]{1,0:T(8,128)(2,1)}, bf16[768,1024]{1,0:T(8,128)(2,1)}, bf16[768,1024]{1,0:T(8,128)(2,1)}) fusion(f32[768]{0:T(1024)S(1)} %broadcast_multiply_fusion, f32[768,1024]{1,0:T(8,128)S(1)} %reshape.70, f32[1024]{0:T(1024)S(1)} %copy-done, bf16[768,1024]{1,0:T(8,128)(2,1)} %param.13, f32[768]{0:T(1024)S(1)} %add_rsqrt_fusion, ...), kind=kLoop, calls=%fused_computation.148 | loop fusion | flops 9437184 | bytes 9448192 | tf_op jit(solution)/shard_map/convert_element_type | solution.py:79
  78.8 2.6 %convert_element_type.77 = bf16[96,8192]{1,0:T(8,128)(2,1)S(1)} reshape(bf16[768,1024]{1,0:T(8,128)(2,1)} %get-tuple-element.7) | data formatting | bytes 3145728 | tf_op jit(solution)/shard_map/convert_element_type | solution.py:79
  81.3 0.3 fusion.3
  81.7 16.1 %all_to_all.24 = bf16[4,8,8192]{2,1,0:T(8,128)(2,1)S(1)} all-to-all(bf16[4,8,8192]{2,1,0:T(8,128)(2,1)S(1)} %fusion.3), channel_id=1, replica_groups=mesh['grp'=4,'tp'=8] {'grp'}, dimensions={0} | all-to-all | bytes 1048576 | tf_op jit(solution)/shard_map/all_to_all | solution.py:83
  97.8 0.3 convolution_convert_fusion.2
  98.1 0.2 reshape.69
  98.4 9.5 %convolution_convert_fusion = bf16[256,8192]{1,0:T(8,128)(2,1)} fusion(bf16[256,1024]{1,0:T(8,128)(2,1)S(1)} %reshape.69, bf16[8192,1024]{1,0:T(8,128)(2,1)} %param.8), kind=kOutput, calls=%fused_computation.3 | convolution fusion | flops 4297064448 | bytes 21495808 | tf_op jit(solution)/shard_map/dot_general | solution.py:88
  107.9 0.0 reduce-scatter.2.cloned.1.call-update
  107.9 49.7 %reduce-scatter.2.cloned.1.call-done = bf16[256,1024]{1,0:T(8,128)(2,1)} async-done(((bf16[256,8192]{1,0:T(8,128)(2,1)}), bf16[256,1024]{1,0:T(8,128)(2,1)}) %reduce-scatter.2.cloned.1.call-update) | async-done | bytes 524304 | tf_op jit(solution)/shard_map/reduce_scatter | solution.py:91
  157.6 2.5 %fusion.80 = bf16[256,1024]{1,0:T(8,128)(2,1)} fusion(bf16[256,1024]{1,0:T(8,128)(2,1)} %reduce-scatter.2.cloned.1.call-done, bf16[256,8192]{1,0:T(8,128)(2,1)} %param.7, s32[]{:T(128)S(6)} %select_n.41), kind=kLoop, calls=%fused_computation.94 | loop fusion | flops 3145728 | bytes 1572868 | tf_op jit(solution)/shard_map/convert_element_type | solution.py:97
  (3 shorter events, 0.0 us)
Async XLA Ops:
  32.4 27.0 %copy-start = (f32[1024]{0:T(1024)S(1)}, f32[1024]{0:T(1024)}, u32[]{:S(2)}) copy-start(f32[1024]{0:T(1024)} %param.12) | copy-start | bytes 12292
  33.5 20.8 %all-to-all-start = ((bf16[4,8,8192]{2,1,0:T(8,128)(2,1)}), bf16[4,8,8192]{2,1,0:T(8,128)(2,1)S(1)}, u32[]{:S(2)}, u32[]{:S(2)}) async-start(bf16[4,8,8192]{2,1,0:T(8,128)(2,1)} %fusion.2), calls=%async_computation | async-start | bytes 1048576 | tf_op jit(solution)/shard_map/all_to_all | solution.py:56
  39.8 117.8 %reduce-scatter.2.cloned.1.call-start = ((), (), s32[]{:S(2)}) async-start(), calls=%async_computation.3 | async-start | bytes 4718592 | tf_op jit(solution)/shard_map/reduce_scatter | solution.py:91
Sparse Core Ops, SparseCore 0:
  108.0 49.5 reduce-scatter.1
where the time goes:
time: 167 us
  waiting for transfers between devices  61.2 us (37%)
  matrix products  37.7 us (23%)
  blocking collectives  29.2 us (17%)
  between operations  14.1 us (8%)
  other arithmetic  9.58 us (6%)
  local copies, waits for them, and re-layouts  8.8 us (5%)
  starting transfers between devices  6.31 us (4%)
    reduce_scatter x1, waiting for transfers between devices, on_device(): lax.psum_scatter(partial_grads.astype(jnp.bfloat16), 'tp', scatter_dimens...  49.7 us
    dot_general x1, matrix products, on_device(): jnp.dot(activated, proj_weight, preferred_element_type=jnp.float32)  24 us
    all_to_all x1, blocking collectives, on_device(): lax.all_to_all(back_out, 'grp', split_axis=0, concat_axis=0, tiled=True)  16.1 us
    psum x1, blocking collectives, on_device(): lax.psum((jnp.sum(wide_merged * wide_merged, axis=1), jnp.sum(grad_in * w...  13.1 us
    all_to_all x1, waiting for transfers between devices, on_device(): lax.all_to_all(outgoing, 'grp', split_axis=0, concat_axis=0, tiled=True)  11.5 us
    dot_general x1, matrix products, on_device(): lax.dot_general(d_image, proj_weight, (((1,), (1,)), ((), ())), preferred...  9.53 us
    all_to_all x1, starting transfers between devices, on_device(): lax.all_to_all(outgoing, 'grp', split_axis=0, concat_axis=0, tiled=True)  6.3 us
    convert_element_type x1, other arithmetic, on_device(): d_image_tiles = d_tiles.astype(jnp.bfloat16)  4.02 us
  transfers between devices with their start and end apart: 2, of which 2 were waited for; matrix products, arithmetic and copies ran while one was open for 2% of the time, Pallas kernels for 0%

commit v1 on v0

v1 whole, which is shorter than its diff:
```python
import functools

import jax
import jax.numpy as jnp
from jax import lax
from jax.experimental import pallas as pl
from jax.experimental.pallas import tpu as pltpu
from jax.sharding import PartitionSpec as P

TILE = 8
STRIP = 2 * TILE
LANES = 128
MESH = pl.DeviceIdType.MESH
F32 = jnp.float32
BF16 = jnp.bfloat16

epsilon = 1e-05


def normal_cdf(values):
    return 0.5 * (1.0 + lax.erf(values * 0.7071067811865476))


def gelu_slope(values):
    density = jnp.exp(-0.5 * values * values) * 0.3989422804014327
    return normal_cdf(values) + values * density


def tile_maps(tile_pos, groups, tiles_dev, spread, capacity):
    group_index = lax.axis_index("grp")
    slots = groups * capacity
    tile_index = jnp.arange(tile_pos.shape[0], dtype=jnp.int32)
    source = tile_index // tiles_dev
    target = tile_pos // spread
    local_pos = tile_pos - group_index * spread
    earlier = (
        (source[:, None] == source[None, :])
        & (target[:, None] == target[None, :])
        & (tile_index[None, :] < tile_index[:, None])
    )
    standing = jnp.sum(earlier.astype(jnp.int32), axis=1)
    arrive = source * capacity + standing
    here = target == group_index
    slot_index = jnp.arange(slots, dtype=jnp.int32)
    needed = jnp.sum(
        jnp.where(here[None, :] & (arrive[None, :] == slot_index[:, None]), local_pos[None, :], 0),
        axis=1,
    )
    depart = target * capacity + standing
    mine = source == group_index
    own_slot = lax.dynamic_slice_in_dim(depart, group_index * tiles_dev, tiles_dev, 0)
    tile_of_slot = jnp.sum(
        jnp.where(
            mine[None, :] & (depart[None, :] == slot_index[:, None]),
            (tile_index - group_index * tiles_dev)[None, :],
            0,
        ),
        axis=1,
    )
    hits = local_pos[None, :] == jnp.arange(spread, dtype=jnp.int32)[:, None]
    place = jnp.sum(jnp.where(hits, arrive[None, :] + 1, 0), axis=1) - 1
    return jnp.concatenate([needed, own_slot, tile_of_slot, place])


def halving_plan(lanes):
    bits = lanes.bit_length() - 1
    orders = (list(range(1, bits)), list(range(bits - 1, 0, -1)))
    plan = []
    for order in orders:
        kept = [rel for rel in range(lanes) if rel % 2 == 0]
        stages = []
        number = 0
        for bit in order:
            sent = [rel for rel in kept if (rel >> bit) & 1]
            kept = [rel for rel in kept if not (rel >> bit) & 1]
            stages.append((bit, {rel: number + place for place, rel in enumerate(sent)}))
            number += len(sent)
        plan.append(stages)
    return plan


def kernel(
    groups, lanes, capacity,
    maps, hidden, weight, bias, gain, text, d_normed,
    normed_out, d_text_out, d_hidden_out,
    hid_v, w_v, act_v, acc_v, img_v, d_img_v, text_v, dn_v, normed_v, d_text_v, d_hid_v,
    send_dn, recv_dn, n_img, send_n, recv_n,
    stat_i, stat_x, row_i, row_x, got_i, got_x, coef_i, coef_x,
    part, first, later,
    load_sem, hid_sem, w_sem, out_sem,
    dn_s, dn_r, n_s, n_r, si_s, si_r, sx_s, sx_r, f_s, f_r, l_s, l_r,
):
    grp = lax.axis_index("grp")
    tp = lax.axis_index("tp")
    rows, cols = img_v.shape
    spread = text_v.shape[0]
    tiles_dev = rows // TILE
    slots = groups * capacity
    width = cols * lanes
    half = rows // 2
    piece = cols // 2 if cols % (2 * LANES) == 0 else cols
    at_slot, at_tile, at_place = slots, slots + tiles_dev, 2 * slots + tiles_dev

    def hid_copy(k):
        return pltpu.make_async_copy(
            hidden.at[:, pl.ds(pl.multiple_of(k * cols, cols), cols)], hid_v.at[k], hid_sem.at[k]
        )

    def w_copy(k):
        return pltpu.make_async_copy(
            weight.at[pl.ds(pl.multiple_of(k * cols, cols), cols), :], w_v.at[k], w_sem.at[k]
        )

    dn_copy = pltpu.make_async_copy(d_normed, dn_v, load_sem.at[0])
    text_copy = pltpu.make_async_copy(text, text_v, load_sem.at[1])
    dn_copy.start()
    hid_copy(0).start()
    w_copy(0).start()
    text_copy.start()
    for k in range(1, lanes):
        hid_copy(k).start()
        w_copy(k).start()

    barrier = pltpu.get_barrier_semaphore()
    for d in range(1, groups):
        pl.semaphore_signal(
            barrier, inc=1, device_id={"grp": (grp + d) % groups}, device_id_type=MESH
        )
    for d in range(1, lanes):
        pl.semaphore_signal(
            barrier, inc=1, device_id={"tp": (tp + d) % lanes}, device_id_type=MESH
        )

    def to_group(source, target, send, receive):
        copies = []
        for d in range(1, groups):
            peer = (grp + d) % groups
            copies.append(
                pltpu.make_async_remote_copy(
                    src_ref=source.at[pl.ds(peer * capacity, capacity)],
                    dst_ref=target.at[pl.ds(grp * capacity, capacity)],
                    send_sem=send.at[d - 1],
                    recv_sem=receive.at[d - 1],
                    device_id={"grp": peer},
                    device_id_type=MESH,
                )
            )
        return copies

    def to_lanes(source, target, send, receive):
        return [
            pltpu.make_async_remote_copy(
                src_ref=source,
                dst_ref=target.at[d - 1],
                send_sem=send.at[d - 1],
                recv_sem=receive.at[d - 1],
                device_id={"tp": (tp + d) % lanes},
                device_id_type=MESH,
            )
            for d in range(1, lanes)
        ]

    dn_copy.wait()

    @pl.loop(0, slots)
    def _(q):
        send_dn[q] = dn_v[maps[q]]

    @pl.loop(0, capacity)
    def _(k):
        recv_dn[grp * capacity + k] = dn_v[maps[grp * capacity + k]]

    pl.semaphore_wait(barrier, groups + lanes - 2)
    dn_copies = to_group(send_dn, recv_dn, dn_s, dn_r)
    for copy in dn_copies:
        copy.start()

    gains = gain[...]
    lane = lax.broadcasted_iota(jnp.int32, (STRIP, LANES), 1)

    def row_sums(values, grads):
        squares = jnp.sum(values * values, axis=1, keepdims=True)
        crosses = jnp.sum(grads * values, axis=1, keepdims=True)
        return jnp.where(lane == 0, squares, jnp.where(lane == 1, crosses, 0.0))

    def doc_strip(ref, j):
        return ref[pl.ds(2 * j, 2)].astype(F32).reshape(STRIP, cols)

    text_copy.wait()

    @pl.loop(0, spread // 2)
    def _(j):
        grads = doc_strip(dn_v, j) * gains
        stat_x[pl.ds(pl.multiple_of(j * STRIP, STRIP), STRIP), :] = row_sums(
            doc_strip(text_v, j), grads
        )

    row_x[...] = stat_x[...].T[:TILE, :]
    x_copies = to_lanes(row_x, got_x, sx_s, sx_r)
    for copy in x_copies:
        copy.start()

    acc_v[...] = jnp.zeros_like(acc_v)

    @pl.loop(0, lanes)
    def _(k):
        hid_copy(k).wait()

        @pl.loop(0, rows // STRIP)
        def _(j):
            strip = pl.ds(pl.multiple_of(j * STRIP, STRIP), STRIP)
            values = hid_v[k, strip, :].astype(F32)
            act_v[strip, :] = (values * normal_cdf(values)).astype(BF16)

        w_copy(k).wait()

        @pl.loop(0, cols // piece)
        def _(n):
            span = pl.ds(pl.multiple_of(n * piece, LANES), piece)
            acc_v[:, span] += jnp.dot(act_v[...], w_v[k, :, span], preferred_element_type=F32)

    for copy in dn_copies:
        copy.wait_recv()

    def grad_strip(j):
        one = recv_dn[maps[at_slot + 2 * j]].astype(F32)
        two = recv_dn[maps[at_slot + 2 * j + 1]].astype(F32)
        return jnp.concatenate([one, two], axis=0) * gains

    biases = bias[...]

    @pl.loop(0, rows // STRIP)
    def _(j):
        strip = pl.ds(pl.multiple_of(j * STRIP, STRIP), STRIP)
        image = (acc_v[strip, :] + biases).astype(BF16)
        img_v[strip, :] = image
        stat_i[strip, :] = row_sums(image.astype(F32), grad_strip(j))

    row_i[...] = stat_i[...].T[:TILE, :]
    i_copies = to_lanes(row_i, got_i, si_s, si_r)
    for copy in i_copies:
        copy.start()

    def coefficients(own, got, copies, target):
        for copy in copies:
            copy.wait_recv()
        total = own[...]
        for d in range(lanes - 1):
            total = total + got[d]
        inverse = lax.rsqrt(total[0:1, :] / width + epsilon)
        second = inverse * inverse * (total[1:2, :] / width)
        count = own.shape[1]
        stacked = jnp.concatenate(
            [
                jnp.broadcast_to(inverse, (TILE, count)),
                jnp.broadcast_to(second, (TILE, count)),
                jnp.zeros((LANES - 2 * TILE, count), F32),
            ],
            axis=0,
        )
        target[...] = stacked.T

    coefficients(row_i, got_i, i_copies, coef_i)

    @pl.loop(0, rows // STRIP)
    def _(j):
        strip = pl.ds(pl.multiple_of(j * STRIP, STRIP), STRIP)
        image = img_v[strip, :].astype(F32)
        inverse = coef_i[strip, 0:1]
        second = coef_i[strip, TILE : TILE + 1]
        d_img_v[strip, :] = (inverse * (grad_strip(j) - image * second)).astype(BF16)
        n_img[pl.ds(2 * j, 2)] = (image * inverse * gains).reshape(2, TILE, cols).astype(BF16)

    @pl.loop(0, slots)
    def _(q):
        send_n[q] = n_img[maps[at_tile + q]]

    @pl.loop(0, capacity)
    def _(k):
        recv_n[grp * capacity + k] = n_img[maps[at_tile + grp * capacity + k]]

    n_copies = to_group(send_n, recv_n, n_s, n_r)
    for copy in n_copies:
        copy.start()

    bit_steps = []
    left = tp
    for bit in range(lanes.bit_length() - 1):
        bit_steps.append((1 - 2 * (left % 2)) * (1 << bit))
        left = left // 2
    plan = halving_plan(lanes)

    def block_of(rel):
        block = tp
        for bit, step in enumerate(bit_steps):
            if (rel >> bit) & 1:
                block = block + step
        return block

    def product(rel, add):
        block = block_of(rel)

        @pl.loop(0, cols // piece)
        def _(n):
            span = pl.ds(pl.multiple_of(n * piece, LANES), piece)
            value = lax.dot_general(
                d_img_v[...], w_v[block, span, :], (((1,), (1,)), ((), ())),
                preferred_element_type=F32,
            )
            if add is not None:
                value = value + first[add, :, span].astype(F32)
            part[rel, :, span] = value.astype(BF16)

    def first_copy(rel):
        return pltpu.make_async_remote_copy(
            src_ref=part.at[rel],
            dst_ref=first.at[rel // 2],
            send_sem=f_s.at[rel // 2],
            recv_sem=f_r.at[rel // 2],
            device_id={"tp": tp + bit_steps[0]},
            device_id_type=MESH,
        )

    def later_copy(side, bit, rel, number):
        return pltpu.make_async_remote_copy(
            src_ref=part.at[rel, pl.ds(side * half, half), :],
            dst_ref=later.at[side, number],
            send_sem=l_s.at[side, number],
            recv_sem=l_r.at[side, number],
            device_id={"tp": tp + bit_steps[bit]},
            device_id_type=MESH,
        )

    urgent = sorted(range(0, lanes, 2), key=lambda rel: (-bin(rel).count("1"), -rel))
    first_copies = {}
    later_copies = {}
    for rel in urgent:
        product(rel + 1, None)
        first_copies[rel] = first_copy(rel + 1)
        first_copies[rel].start()

    def send_on(side, stage, rel):
        if stage < len(plan[side]) and rel in plan[side][stage][1]:
            bit, numbers = plan[side][stage]
            copy = later_copy(side, bit, rel, numbers[rel])
            later_copies[side, numbers[rel]] = copy
            copy.start()

    for rel in urgent:
        first_copies[rel].wait_recv()
        product(rel, rel // 2)
        for side in range(2):
            send_on(side, 0, rel)

    coefficients(row_x, got_x, x_copies, coef_x)

    @pl.loop(0, spread // 2)
    def _(j):
        strip = pl.ds(pl.multiple_of(j * STRIP, STRIP), STRIP)
        values = doc_strip(text_v, j)
        grads = doc_strip(dn_v, j) * gains
        inverse = coef_x[strip, 0:1]
        second = coef_x[strip, TILE : TILE + 1]
        normed_v[pl.ds(2 * j, 2)] = (
            (values * inverse * gains).reshape(2, TILE, cols).astype(BF16)
        )
        d_values = inverse * (grads - values * second)
        for side in range(2):
            flag = jnp.full((TILE, cols), maps[at_place + 2 * j + side], jnp.int32)
            d_text_v[2 * j + side] = jnp.where(
                flag >= 0, 0.0, d_values[side * TILE : (side + 1) * TILE, :]
            ).astype(BF16)

    d_text_copy = pltpu.make_async_copy(d_text_v, d_text_out, out_sem.at[0])
    d_text_copy.start()

    @pl.loop(0, rows // STRIP)
    def _(j):
        strip = pl.ds(pl.multiple_of(j * STRIP, STRIP), STRIP)
        acc_v[strip, :] = gelu_slope(hid_v[tp, strip, :].astype(F32))

    def collect(stage, last):
        for side in range(2):
            if stage >= len(plan[side]):
                continue
            bit, numbers = plan[side][stage]
            ahead = plan[side][stage + 1][1] if stage + 1 < len(plan[side]) else {}
            goal = sorted(numbers, key=lambda rel: (rel - (1 << bit)) not in ahead)
            for rel in goal:
                number = numbers[rel]
                mine = rel - (1 << bit)
                later_copies[side, number].wait_recv()
                if mine:

                    @pl.loop(0, half // STRIP)
                    def _(j):
                        here = pl.multiple_of(j * STRIP, STRIP)
                        there = pl.ds(side * half + here, STRIP)
                        part[mine, there, :] = (
                            part[mine, there, :].astype(F32)
                            + later[side, number, pl.ds(here, STRIP), :].astype(F32)
                        ).astype(BF16)

                    send_on(side, stage + 1, mine)

    stages = len(plan[0])
    for stage in range(stages - 1):
        collect(stage, False)

    for copy in n_copies:
        copy.wait_recv()

    @pl.loop(0, spread)
    def _(p):
        slot = maps[at_place + p]
        flag = jnp.full((TILE, cols), slot, jnp.int32)
        normed_v[p] = jnp.where(
            flag >= 0, recv_n[jnp.maximum(slot, 0)].astype(F32), normed_v[p].astype(F32)
        ).astype(BF16)

    normed_copy = pltpu.make_async_copy(normed_v, normed_out, out_sem.at[1])
    normed_copy.start()
    if stages:
        collect(stages - 1, True)

    for side in range(2):
        tails = [numbers[1 << bit] for bit, numbers in plan[side]]

        @pl.loop(0, half // STRIP)
        def _(j):
            here = pl.multiple_of(j * STRIP, STRIP)
            there = pl.ds(side * half + here, STRIP)
            total = part[0, there, :].astype(F32)
            for number in tails:
                total = total + later[side, number, pl.ds(here, STRIP), :].astype(F32)
            d_hid_v[there, :] = (total * acc_v[there, :]).astype(BF16)

    d_hidden_copy = pltpu.make_async_copy(d_hid_v, d_hidden_out, out_sem.at[2])
    d_hidden_copy.start()
    for copy in dn_copies + x_copies + i_copies + n_copies:
        copy.wait_send()
    for copy in list(first_copies.values()) + list(later_copies.values()):
        copy.wait_send()
    d_text_copy.wait()
    normed_copy.wait()
    d_hidden_copy.wait()


def on_device(hidden, proj_weight, proj_bias, tile_pos, text_embed, norm_gain, d_normed):
    rows, width = hidden.shape
    cols = proj_weight.shape[1]
    tokens = text_embed.shape[0]
    groups = lax.axis_size("grp")
    lanes = lax.axis_size("tp")
    assert lanes >= 2 and lanes & (lanes - 1) == 0, lanes
    tiles_dev = rows // TILE
    spread = tokens // TILE
    capacity = max(2, (tiles_dev + groups - 1) // groups)
    slots = groups * capacity
    maps = tile_maps(tile_pos, groups, tiles_dev, spread, capacity)
    any_spec = pl.BlockSpec(memory_space=pl.ANY)
    vmem_spec = pl.BlockSpec(memory_space=pltpu.VMEM)
    half = rows // 2
    kept = max(1, lanes // 2 - 1)

    def vmem(*shape, dtype=BF16):
        return pltpu.VMEM(shape, dtype)

    def sems(*shape):
        return pltpu.SemaphoreType.DMA(shape)

    tiled = (spread, TILE, cols)
    normed, d_text, d_hidden = pl.pallas_call(
        functools.partial(kernel, groups, lanes, capacity),
        out_shape=(
            jax.ShapeDtypeStruct(tiled, BF16),
            jax.ShapeDtypeStruct(tiled, BF16),
            jax.ShapeDtypeStruct((rows, cols), BF16),
        ),
        in_specs=[
            pl.BlockSpec(memory_space=pltpu.SMEM),
            any_spec, any_spec, vmem_spec, vmem_spec, any_spec, any_spec,
        ],
        out_specs=(any_spec, any_spec, any_spec),
        scratch_shapes=[
            vmem(lanes, rows, cols),
            vmem(lanes, cols, cols),
            vmem(rows, cols),
            vmem(rows, cols, dtype=F32),
            vmem(rows, cols),
            vmem(rows, cols),
            vmem(*tiled),
            vmem(*tiled),
            vmem(*tiled),
            vmem(*tiled),
            vmem(rows, cols),
            vmem(slots, TILE, cols),
            vmem(slots, TILE, cols),
            vmem(tiles_dev, TILE, cols),
            vmem(slots, TILE, cols),
            vmem(slots, TILE, cols),
            vmem(rows, LANES, dtype=F32),
            vmem(tokens, LANES, dtype=F32),
            vmem(TILE, rows, dtype=F32),
            vmem(TILE, tokens, dtype=F32),
            vmem(lanes - 1, TILE, rows, dtype=F32),
            vmem(lanes - 1, TILE, tokens, dtype=F32),
            vmem(rows, LANES, dtype=F32),
            vmem(tokens, LANES, dtype=F32),
            vmem(lanes, rows, cols),
            vmem(lanes // 2, rows, cols),
            vmem(2, kept, half, cols),
            sems(2), sems(lanes), sems(lanes), sems(3),
            sems(groups - 1), sems(groups - 1), sems(groups - 1), sems(groups - 1),
            sems(lanes - 1), sems(lanes - 1), sems(lanes - 1), sems(lanes - 1),
            sems(lanes // 2), sems(lanes // 2), sems(2, kept), sems(2, kept),
        ],
        compiler_params=pltpu.CompilerParams(
            collective_id=0, has_side_effects=True, vmem_limit_bytes=58 * 1024 * 1024
        ),
        cost_estimate=pl.CostEstimate(
            flops=4 * rows * width * cols,
            bytes_accessed=2 * (width * cols + rows * width + 5 * tokens * cols),
            transcendentals=rows * width,
        ),
        name="projector_norm",
    )(
        maps, hidden, proj_weight, proj_bias.reshape(1, cols), norm_gain.reshape(1, cols),
        text_embed.reshape(tiled), d_normed.reshape(tiled),
    )
    return (normed.reshape(tokens, cols), d_text.reshape(tokens, cols), d_hidden)


def solution(mesh):
    in_specs = (
        P("grp", None),
        P(None, "tp"),
        P("tp"),
        P(),
        P("grp", "tp"),
        P("tp"),
        P("grp", "tp"),
    )
    out_specs = (P("grp", "tp"), P("grp", "tp"), P("grp", "tp"))
    return jax.shard_map(
        on_device, mesh=mesh, in_specs=in_specs, out_specs=out_specs, check_vma=False
    )
```

time: 167 us -> 67.3 us (0.40)
  waiting for transfers between devices: 61.2 us -> 0 us
  Pallas kernels: 0 us -> 58.8 us
  matrix products: 37.7 us -> 0 us
  blocking collectives: 29.2 us -> 0 us
  between operations: 14.1 us -> 0.68 us
  other arithmetic: 9.58 us -> 2.51 us
  starting transfers between devices: 6.31 us -> 0 us
  local copies, waits for them, and re-layouts: 8.8 us -> 5.06 us
    pallas_call x0 -> x1, Pallas kernels: none -> 58.8 us  [on_device(): pl.pallas_call(functools.partial(kernel, groups, lanes, capacity), out_sh...]
    reduce_scatter x1 -> x0, waiting for transfers between devices: 49.7 us -> none  [on_device(): lax.psum_scatter(partial_grads.astype(jnp.bfloat16), 'tp', scatter_dimens...]
    dot_general x7 -> x0, matrix products: 37.7 us -> none  [the longest x1 24 us: on_device(): jnp.dot(activated, proj_weight, preferred_element_type=jnp.float32)]
    all_to_all x1 -> x0, blocking collectives: 16.1 us -> none  [on_device(): lax.all_to_all(back_out, 'grp', split_axis=0, concat_axis=0, tiled=True)]
    psum x1 -> x0, blocking collectives: 13.1 us -> none  [on_device(): lax.psum((jnp.sum(wide_merged * wide_merged, axis=1), jnp.sum(grad_in * w...]
    all_to_all x1 -> x0, waiting for transfers between devices: 11.5 us -> none  [on_device(): lax.all_to_all(outgoing, 'grp', split_axis=0, concat_axis=0, tiled=True)]
    convert_element_type x2 -> x0, other arithmetic: 6.51 us -> none  [the longest x1 4.02 us: on_device(): d_image_tiles = d_tiles.astype(jnp.bfloat16)]
    all_to_all x1 -> x0, starting transfers between devices: 6.3 us -> none  [on_device(): lax.all_to_all(outgoing, 'grp', split_axis=0, concat_axis=0, tiled=True)]
  transfers between devices with their start and end apart: 2 -> 0, of which waited for: 2 -> 0; matrix products, arithmetic and copies ran while one was open for 2% -> 0% of each run, Pallas kernels for 0% -> 0%
where the time goes in v1:
time: 67.3 us; the launch traced here: 67.1 us
  Pallas kernels  58.8 us (87%)
  local copies, waits for them, and re-layouts  5.06 us (8%)
  other arithmetic  2.51 us (4%)
  between operations  0.68 us (1%)
    pallas_call x1, Pallas kernels, on_device(): pl.pallas_call(functools.partial(kernel, groups, lanes, capacity), out_sh...  58.8 us
    unnamed x7, local copies, waits for them, and re-layouts  4.98 us

profile of v1, /device:TPU:0, one launch (start us, length us, event | category | flops | bytes accessed | tf_op | source)
XLA Modules:
  0.0 67.1 jit_solution(2415087685675287314)
XLA Ops:
  0.6 0.7 broadcast_subtract_fusion
  1.3 0.7 broadcast_compare_fusion.1
  2.0 0.2 convert_reduce_fusion
  2.2 0.1 select_reduce_fusion.1
  2.3 0.1 dynamic_slice.3
  2.4 0.1 select_reduce_fusion.2
  2.5 0.1 select_reduce_fusion
  2.6 0.6 pad_add_fusion.maps
  3.2 58.8 %projector_norm.1 = (bf16[96,8,1024]{2,1,0:T(8,128)(2,1)}, bf16[96,8,1024]{2,1,0:T(8,128)(2,1)}, bf16[256,1024]{1,0:T(8,128)(2,1)}) custom-call(s32[192]{0:T(256)} %pad_add_fusion.maps, bf16[256,8192]{1,0:T(8,128)(2,1)} %hidden.1, bf16[8192,1024]{1,0:T(8,128)(2,1)} %weight.1, f32[1,1024]{1,0:T(1,128)} %bitcast.10, f32[1,1024]{1,0:T(1,128)} %bitcast.11, ...), custom_call_target="tpu_custom_call" | custom-call | flops 8589934592 | bytes 28835840 | tf_op jit(solution)/shard_map/projector_norm/pallas_call | solution.py:473
  62.1 0.0 copy-start
  62.1 2.8 %copy.13 = bf16[768,1024]{1,0:T(8,128)(2,1)} copy(bf16[768,1024]{1,0:T(8,128)(2,1)} %bitcast.7) | data formatting | bytes 3145728
  64.9 0.0 copy-done
  64.9 0.0 copy-start.1
  64.9 1.1 %copy.14 = bf16[768,1024]{1,0:T(8,128)(2,1)} copy(bf16[768,1024]{1,0:T(8,128)(2,1)S(1)} %bitcast.6) | data formatting | bytes 3145728
  66.0 0.3 copy-done.1
  66.3 0.8 %copy.15 = bf16[256,1024]{1,0:T(8,128)(2,1)} copy(bf16[256,1024]{1,0:T(8,128)(2,1)S(1)} %copy-done.1) | data formatting | bytes 1048576
  (4 shorter events, 0.0 us)
Async XLA Ops:
  62.1 2.8 %copy-start = (bf16[96,8,1024]{2,1,0:T(8,128)(2,1)S(1)}, bf16[96,8,1024]{2,1,0:T(8,128)(2,1)}, u32[]{:S(2)}) copy-start(bf16[96,8,1024]{2,1,0:T(8,128)(2,1)} %get-tuple-element.7) | copy-start | bytes 4718596
  64.9 1.4 %copy-start.1 = (bf16[256,1024]{1,0:T(8,128)(2,1)S(1)}, bf16[256,1024]{1,0:T(8,128)(2,1)}, u32[]{:S(2)}) copy-start(bf16[256,1024]{1,0:T(8,128)(2,1)} %get-tuple-element.20) | copy-start | bytes 1572868

commit v2 on v1

--- a/solution.py
+++ b/solution.py
@@ -31,7 +31,7 @@
     slots = groups * capacity
     tile_index = jnp.arange(tile_pos.shape[0], dtype=jnp.int32)
     source = tile_index // tiles_dev
-    target = tile_pos // spread
+    target = lax.div(tile_pos, jnp.int32(spread))
     local_pos = tile_pos - group_index * spread
     earlier = (
         (source[:, None] == source[None, :])
@@ -82,12 +82,12 @@
 def kernel(
     groups, lanes, capacity,
     maps, hidden, weight, bias, gain, text, d_normed,
-    normed_out, d_text_out, d_hidden_out,
-    hid_v, w_v, act_v, acc_v, img_v, d_img_v, text_v, dn_v, normed_v, d_text_v, d_hid_v,
+    normed_v, d_text_v, d_hid_v,
+    hid_v, w_v, act_v, act_got, acc_v, img_v, d_img_v, text_v, dn_v,
     send_dn, recv_dn, n_img, send_n, recv_n,
     stat_i, stat_x, row_i, row_x, got_i, got_x, coef_i, coef_x,
     part, first, later,
-    load_sem, hid_sem, w_sem, out_sem,
+    load_sem, hid_sem, w_sem, a_s, a_r,
     dn_s, dn_r, n_s, n_r, si_s, si_r, sx_s, sx_r, f_s, f_r, l_s, l_r,
 ):
     grp = lax.axis_index("grp")
@@ -101,25 +101,35 @@
     piece = cols // 2 if cols % (2 * LANES) == 0 else cols
     at_slot, at_tile, at_place = slots, slots + tiles_dev, 2 * slots + tiles_dev
 
+    odd = tp % 2
+    pairs = lanes // 2
+
     def hid_copy(k):
         return pltpu.make_async_copy(
-            hidden.at[:, pl.ds(pl.multiple_of(k * cols, cols), cols)], hid_v.at[k], hid_sem.at[k]
-        )
-
-    def w_copy(k):
+            hidden.at[:, pl.ds(pl.multiple_of((2 * k + odd) * cols, cols), cols)],
+            hid_v.at[k],
+            hid_sem.at[k],
+        )
+
+    def w_copy(k, other):
+        block = 2 * k + (1 - odd if other else odd)
         return pltpu.make_async_copy(
-            weight.at[pl.ds(pl.multiple_of(k * cols, cols), cols), :], w_v.at[k], w_sem.at[k]
+            weight.at[pl.ds(pl.multiple_of(block * cols, cols), cols), :],
+            w_v.at[block],
+            w_sem.at[2 * k + other],
         )
 
     dn_copy = pltpu.make_async_copy(d_normed, dn_v, load_sem.at[0])
     text_copy = pltpu.make_async_copy(text, text_v, load_sem.at[1])
     dn_copy.start()
     hid_copy(0).start()
-    w_copy(0).start()
+    w_copy(0, 0).start()
+    for k in range(1, pairs):
+        hid_copy(k).start()
+        w_copy(k, 0).start()
+        w_copy(k - 1, 1).start()
+    w_copy(pairs - 1, 1).start()
     text_copy.start()
-    for k in range(1, lanes):
-        hid_copy(k).start()
-        w_copy(k).start()
 
     barrier = pltpu.get_barrier_semaphore()
     for d in range(1, groups):
@@ -186,38 +196,69 @@
     def doc_strip(ref, j):
         return ref[pl.ds(2 * j, 2)].astype(F32).reshape(STRIP, cols)
 
-    text_copy.wait()
-
-    @pl.loop(0, spread // 2)
-    def _(j):
-        grads = doc_strip(dn_v, j) * gains
-        stat_x[pl.ds(pl.multiple_of(j * STRIP, STRIP), STRIP), :] = row_sums(
-            doc_strip(text_v, j), grads
-        )
-
-    row_x[...] = stat_x[...].T[:TILE, :]
-    x_copies = to_lanes(row_x, got_x, sx_s, sx_r)
-    for copy in x_copies:
-        copy.start()
-
-    acc_v[...] = jnp.zeros_like(acc_v)
-
-    @pl.loop(0, lanes)
-    def _(k):
-        hid_copy(k).wait()
-
-        @pl.loop(0, rows // STRIP)
-        def _(j):
-            strip = pl.ds(pl.multiple_of(j * STRIP, STRIP), STRIP)
-            values = hid_v[k, strip, :].astype(F32)
-            act_v[strip, :] = (values * normal_cdf(values)).astype(BF16)
-
-        w_copy(k).wait()
-
-        @pl.loop(0, cols // piece)
+    bit_steps = []
+    left = tp
+    for bit in range(lanes.bit_length() - 1):
+        bit_steps.append((1 - 2 * (left % 2)) * (1 << bit))
+        left = left // 2
+
+    act_copies = [
+        pltpu.make_async_remote_copy(
+            src_ref=act_v.at[k],
+            dst_ref=act_got.at[k],
+            send_sem=a_s.at[k],
+            recv_sem=a_r.at[k],
+            device_id={"tp": tp + bit_steps[0]},
+            device_id_type=MESH,
+        )
+        for k in range(pairs)
+    ]
+    steps = min(4, cols // LANES)
+    span_width = cols // steps
+    strips = rows // STRIP // steps
+
+    def forward(k, ready):
+        if k is not None:
+            hid_copy(k).wait()
+        for source, other in ready:
+            w_copy(source, other).wait()
+            if other:
+                act_copies[source].wait_recv()
+
+        @pl.loop(0, steps)
         def _(n):
-            span = pl.ds(pl.multiple_of(n * piece, LANES), piece)
-            acc_v[:, span] += jnp.dot(act_v[...], w_v[k, :, span], preferred_element_type=F32)
+            if k is not None:
+                for j in range(strips):
+                    strip = pl.ds(pl.multiple_of((n * strips + j) * STRIP, STRIP), STRIP)
+                    values = hid_v[k, strip, :].astype(F32)
+                    act_v[k, strip, :] = (values * normal_cdf(values)).astype(BF16)
+            if ready:
+                span = pl.ds(pl.multiple_of(n * span_width, LANES), span_width)
+                total = None if ready[0] == (0, 0) else acc_v[:, span]
+                for source, other in ready:
+                    block = 2 * source + (1 - odd if other else odd)
+                    left_side = act_got[source] if other else act_v[source]
+                    value = jnp.dot(
+                        left_side, w_v[block, :, span], preferred_element_type=F32
+                    )
+                    total = value if total is None else total + value
+                acc_v[:, span] = total
+
+        if k is not None:
+            act_copies[k].start()
+
+    for k in range(pairs):
+        ready = []
+        if k >= 1:
+            ready.append((k - 1, 0))
+        if k >= 2:
+            ready.append((k - 2, 1))
+        forward(k, ready)
+    tail = [(pairs - 1, 0)]
+    if pairs >= 2:
+        tail.append((pairs - 2, 1))
+    forward(None, tail)
+    forward(None, [(pairs - 1, 1)])
 
     for copy in dn_copies:
         copy.wait_recv()
@@ -239,6 +280,20 @@
     row_i[...] = stat_i[...].T[:TILE, :]
     i_copies = to_lanes(row_i, got_i, si_s, si_r)
     for copy in i_copies:
+        copy.start()
+
+    text_copy.wait()
+
+    @pl.loop(0, spread // 2)
+    def _(j):
+        grads = doc_strip(dn_v, j) * gains
+        stat_x[pl.ds(pl.multiple_of(j * STRIP, STRIP), STRIP), :] = row_sums(
+            doc_strip(text_v, j), grads
+        )
+
+    row_x[...] = stat_x[...].T[:TILE, :]
+    x_copies = to_lanes(row_x, got_x, sx_s, sx_r)
+    for copy in x_copies:
         copy.start()
 
     def coefficients(own, got, copies, target):
@@ -283,11 +338,6 @@
     for copy in n_copies:
         copy.start()
 
-    bit_steps = []
-    left = tp
-    for bit in range(lanes.bit_length() - 1):
-        bit_steps.append((1 - 2 * (left % 2)) * (1 << bit))
-        left = left // 2
     plan = halving_plan(lanes)
 
     def block_of(rel):
@@ -334,11 +384,6 @@
     urgent = sorted(range(0, lanes, 2), key=lambda rel: (-bin(rel).count("1"), -rel))
     first_copies = {}
     later_copies = {}
-    for rel in urgent:
-        product(rel + 1, None)
-        first_copies[rel] = first_copy(rel + 1)
-        first_copies[rel].start()
-
     def send_on(side, stage, rel):
         if stage < len(plan[side]) and rel in plan[side][stage][1]:
             bit, numbers = plan[side][stage]
@@ -346,7 +391,15 @@
             later_copies[side, numbers[rel]] = copy
             copy.start()
 
-    for rel in urgent:
+    def send_first(rel):
+        product(rel + 1, None)
+        first_copies[rel] = first_copy(rel + 1)
+        first_copies[rel].start()
+
+    send_first(urgent[0])
+    for place, rel in enumerate(urgent):
+        if place + 1 < len(urgent):
+            send_first(urgent[place + 1])
         first_copies[rel].wait_recv()
         product(rel, rel // 2)
         for side in range(2):
@@ -371,13 +424,10 @@
                 flag >= 0, 0.0, d_values[side * TILE : (side + 1) * TILE, :]
             ).astype(BF16)
 
-    d_text_copy = pltpu.make_async_copy(d_text_v, d_text_out, out_sem.at[0])
-    d_text_copy.start()
-
     @pl.loop(0, rows // STRIP)
     def _(j):
         strip = pl.ds(pl.multiple_of(j * STRIP, STRIP), STRIP)
-        acc_v[strip, :] = gelu_slope(hid_v[tp, strip, :].astype(F32))
+        acc_v[strip, :] = gelu_slope(hid_v[tp // 2, strip, :].astype(F32))
 
     def collect(stage, last):
         for side in range(2):
@@ -418,8 +468,6 @@
             flag >= 0, recv_n[jnp.maximum(slot, 0)].astype(F32), normed_v[p].astype(F32)
         ).astype(BF16)
 
-    normed_copy = pltpu.make_async_copy(normed_v, normed_out, out_sem.at[1])
-    normed_copy.start()
     if stages:
         collect(stages - 1, True)
 
@@ -435,15 +483,10 @@
                 total = total + later[side, number, pl.ds(here, STRIP), :].astype(F32)
             d_hid_v[there, :] = (total * acc_v[there, :]).astype(BF16)
 
-    d_hidden_copy = pltpu.make_async_copy(d_hid_v, d_hidden_out, out_sem.at[2])
-    d_hidden_copy.start()
-    for copy in dn_copies + x_copies + i_copies + n_copies:
+    for copy in act_copies + dn_copies + x_copies + i_copies + n_copies:
         copy.wait_send()
     for copy in list(first_copies.values()) + list(later_copies.values()):
         copy.wait_send()
-    d_text_copy.wait()
-    normed_copy.wait()
-    d_hidden_copy.wait()
 
 
 def on_device(hidden, proj_weight, proj_bias, tile_pos, text_embed, norm_gain, d_normed):
@@ -473,27 +516,25 @@
     normed, d_text, d_hidden = pl.pallas_call(
         functools.partial(kernel, groups, lanes, capacity),
         out_shape=(
-            jax.ShapeDtypeStruct(tiled, BF16),
-            jax.ShapeDtypeStruct(tiled, BF16),
-            jax.ShapeDtypeStruct((rows, cols), BF16),
+            vmem(*tiled),
+            vmem(*tiled),
+            vmem(rows, cols),
         ),
         in_specs=[
             pl.BlockSpec(memory_space=pltpu.SMEM),
             any_spec, any_spec, vmem_spec, vmem_spec, any_spec, any_spec,
         ],
-        out_specs=(any_spec, any_spec, any_spec),
+        out_specs=(vmem_spec, vmem_spec, vmem_spec),
         scratch_shapes=[
-            vmem(lanes, rows, cols),
+            vmem(lanes // 2, rows, cols),
             vmem(lanes, cols, cols),
-            vmem(rows, cols),
+            vmem(lanes // 2, rows, cols),
+            vmem(lanes // 2, rows, cols),
             vmem(rows, cols, dtype=F32),
             vmem(rows, cols),
             vmem(rows, cols),
             vmem(*tiled),
             vmem(*tiled),
-            vmem(*tiled),
-            vmem(*tiled),
-            vmem(rows, cols),
             vmem(slots, TILE, cols),
             vmem(slots, TILE, cols),
             vmem(tiles_dev, TILE, cols),
@@ -510,7 +551,7 @@
             vmem(lanes, rows, cols),
             vmem(lanes // 2, rows, cols),
             vmem(2, kept, half, cols),
-            sems(2), sems(lanes), sems(lanes), sems(3),
+            sems(2), sems(lanes // 2), sems(lanes), sems(lanes // 2), sems(lanes // 2),
             sems(groups - 1), sems(groups - 1), sems(groups - 1), sems(groups - 1),
             sems(lanes - 1), sems(lanes - 1), sems(lanes - 1), sems(lanes - 1),
             sems(lanes // 2), sems(lanes // 2), sems(2, kept), sems(2, kept),
@@ -521,7 +562,7 @@
         cost_estimate=pl.CostEstimate(
             flops=4 * rows * width * cols,
             bytes_accessed=2 * (width * cols + rows * width + 5 * tokens * cols),
-            transcendentals=rows * width,
+            transcendentals=rows * width // 2,
         ),
         name="projector_norm",
     )(

time: 67.3 us -> 60.5 us (0.90)
  Pallas kernels: 58.8 us -> 53.9 us
  local copies, waits for them, and re-layouts: 5.06 us -> 3.16 us
    pallas_call x1, Pallas kernels: 58.8 us -> 53.9 us  [on_device(): pl.pallas_call(functools.partial(kernel, groups, lanes, capacity), out_sh...]
    unnamed x7 -> x3, local copies, waits for them, and re-layouts: 4.98 us -> 3.08 us
where the time goes in v2:
time: 60.5 us; the launch traced here: 60.3 us
  Pallas kernels  53.9 us (89%)
  local copies, waits for them, and re-layouts  3.16 us (5%)
  other arithmetic  2.51 us (4%)
  between operations  0.67 us (1%)
    pallas_call x1, Pallas kernels, on_device(): pl.pallas_call(functools.partial(kernel, groups, lanes, capacity), out_sh...  53.9 us
    unnamed x3, local copies, waits for them, and re-layouts  3.08 us

profile of v2, /device:TPU:0, one launch (start us, length us, event | category | flops | bytes accessed | tf_op | source)
XLA Modules:
  0.0 60.3 jit_solution(3815214095548759516)
XLA Ops:
  0.6 0.7 %broadcast_subtract_fusion = s32[128]{0:T(128)S(1)} fusion(s32[128]{0:T(128)} %param.10, s32[]{:T(128)S(6)} %mul.21), kind=kLoop, calls=%fused_computation.20 | loop fusion | flops 128 | bytes 1028 | tf_op jit(solution)/shard_map/sub | solution.py:35
  1.3 0.7 %broadcast_compare_fusion.1 = (pred[128]{0:T(512)(128)(4,1)S(1)}, s32[128]{0:T(128)S(1)}, pred[128]{0:T(512)(128)(4,1)S(1)}) fusion(s32[]{:T(128)S(6)} %axis_index.15, s32[128]{0:T(128)} %param.10), kind=kLoop, calls=%fused_computation.23 | loop fusion | flops 1408 | bytes 1284 | tf_op jit(solution)/shard_map/eq | solution.py:43
  2.0 0.2 convert_reduce_fusion
  2.2 0.1 select_reduce_fusion.1
  2.3 0.1 dynamic_slice.3
  2.4 0.1 select_reduce_fusion.2
  2.5 0.1 select_reduce_fusion
  2.6 0.6 %pad_add_fusion.maps = s32[192]{0:T(256)} fusion(s32[96]{0:T(128)S(1)} %broadcast_add_fusion, s32[32]{0:T(128)S(1)} %select_reduce_fusion.1, s32[32]{0:T(128)S(1)} %dynamic_slice.3, s32[32]{0:T(128)S(1)} %select_reduce_fusion.2), kind=kLoop, calls=%fused_computation.12 | loop fusion | flops 576 | bytes 1536 | tf_op jit(solution)/shard_map/concatenate | solution.py:62
  3.2 53.9 %projector_norm.1 = (bf16[96,8,1024]{2,1,0:T(8,128)(2,1)S(1)}, bf16[96,8,1024]{2,1,0:T(8,128)(2,1)S(1)}, bf16[256,1024]{1,0:T(8,128)(2,1)S(1)}) custom-call(s32[192]{0:T(256)} %pad_add_fusion.maps, bf16[256,8192]{1,0:T(8,128)(2,1)} %hidden.1, bf16[8192,1024]{1,0:T(8,128)(2,1)} %weight.1, f32[1,1024]{1,0:T(1,128)} %bitcast.10, f32[1,1024]{1,0:T(1,128)} %bitcast.11, ...), custom_call_target="tpu_custom_call" | custom-call | flops 8589934592 | bytes 28835840 | tf_op jit(solution)/shard_map/projector_norm/pallas_call | solution.py:516
  57.2 1.1 %copy.13 = bf16[768,1024]{1,0:T(8,128)(2,1)} copy(bf16[768,1024]{1,0:T(8,128)(2,1)S(1)} %bitcast.7) | data formatting | bytes 3145728
  58.3 1.1 %copy.14 = bf16[768,1024]{1,0:T(8,128)(2,1)} copy(bf16[768,1024]{1,0:T(8,128)(2,1)S(1)} %bitcast.6) | data formatting | bytes 3145728
  59.5 0.8 %copy.15 = bf16[256,1024]{1,0:T(8,128)(2,1)} copy(bf16[256,1024]{1,0:T(8,128)(2,1)S(1)} %get-tuple-element.17) | data formatting | bytes 1048576
  (4 shorter events, 0.0 us)

commit v3 on v2

--- a/solution.py
+++ b/solution.py
@@ -143,7 +143,7 @@
 
     def to_group(source, target, send, receive):
         copies = []
-        for d in range(1, groups):
+        for d in sorted(range(1, groups), key=lambda d: abs(2 * d - groups)):
             peer = (grp + d) % groups
             copies.append(
                 pltpu.make_async_remote_copy(
@@ -324,19 +324,6 @@
         inverse = coef_i[strip, 0:1]
         second = coef_i[strip, TILE : TILE + 1]
         d_img_v[strip, :] = (inverse * (grad_strip(j) - image * second)).astype(BF16)
-        n_img[pl.ds(2 * j, 2)] = (image * inverse * gains).reshape(2, TILE, cols).astype(BF16)
-
-    @pl.loop(0, slots)
-    def _(q):
-        send_n[q] = n_img[maps[at_tile + q]]
-
-    @pl.loop(0, capacity)
-    def _(k):
-        recv_n[grp * capacity + k] = n_img[maps[at_tile + grp * capacity + k]]
-
-    n_copies = to_group(send_n, recv_n, n_s, n_r)
-    for copy in n_copies:
-        copy.start()
 
     plan = halving_plan(lanes)
 
@@ -396,6 +383,29 @@
         first_copies[rel] = first_copy(rel + 1)
         first_copies[rel].start()
 
+    def normed_tiles():
+        @pl.loop(0, rows // STRIP)
+        def _(j):
+            strip = pl.ds(pl.multiple_of(j * STRIP, STRIP), STRIP)
+            image = img_v[strip, :].astype(F32)
+            inverse = coef_i[strip, 0:1]
+            n_img[pl.ds(2 * j, 2)] = (
+                (image * inverse * gains).reshape(2, TILE, cols).astype(BF16)
+            )
+
+        @pl.loop(0, slots)
+        def _(q):
+            send_n[q] = n_img[maps[at_tile + q]]
+
+        @pl.loop(0, capacity)
+        def _(k):
+            recv_n[grp * capacity + k] = n_img[maps[at_tile + grp * capacity + k]]
+
+        copies = to_group(send_n, recv_n, n_s, n_r)
+        for copy in copies:
+            copy.start()
+        return copies
+
     send_first(urgent[0])
     for place, rel in enumerate(urgent):
         if place + 1 < len(urgent):
@@ -404,6 +414,8 @@
         product(rel, rel // 2)
         for side in range(2):
             send_on(side, 0, rel)
+        if place == 0:
+            n_copies = normed_tiles()
 
     coefficients(row_x, got_x, x_copies, coef_x)
 
@@ -487,6 +499,26 @@
         copy.wait_send()
     for copy in list(first_copies.values()) + list(later_copies.values()):
         copy.wait_send()
+
+
+def hand_out(*refs):
+    count = len(refs) // 2
+    sem = refs[-1]
+    copies = []
+    for number in range(count):
+        source, target = refs[number], refs[count + number]
+        cut = source.shape[0] // 2
+        for side in range(2):
+            span = pl.ds(side * cut, cut)
+            copies.append(
+                pltpu.make_async_copy(
+                    source.at[span], target.at[span], sem.at[2 * number + side]
+                )
+            )
+    for copy in copies:
+        copy.start()
+    for copy in copies:
+        copy.wait()
 
 
 def on_device(hidden, proj_weight, proj_bias, tile_pos, text_embed, norm_gain, d_normed):
@@ -569,6 +601,19 @@
         maps, hidden, proj_weight, proj_bias.reshape(1, cols), norm_gain.reshape(1, cols),
         text_embed.reshape(tiled), d_normed.reshape(tiled),
     )
+    normed, d_text, d_hidden = pl.pallas_call(
+        hand_out,
+        out_shape=(
+            jax.ShapeDtypeStruct(tiled, BF16),
+            jax.ShapeDtypeStruct(tiled, BF16),
+            jax.ShapeDtypeStruct((rows, cols), BF16),
+        ),
+        in_specs=[any_spec] * 3,
+        out_specs=(any_spec,) * 3,
+        scratch_shapes=[sems(6)],
+        compiler_params=pltpu.CompilerParams(vmem_limit_bytes=1024 * 1024),
+        name="hand_out",
+    )(normed, d_text, d_hidden)
     return (normed.reshape(tokens, cols), d_text.reshape(tokens, cols), d_hidden)
 
 

time: 60.5 us -> 58.7 us (0.970)
  local copies, waits for them, and re-layouts: 3.16 us -> 0.08 us
  Pallas kernels: 53.9 us -> 55.2 us
    unnamed x3 -> x0, local copies, waits for them, and re-layouts: 3.08 us -> none
    pallas_call x0 -> x1, Pallas kernels: none -> 1.88 us  [on_device(): pl.pallas_call(hand_out, out_shape=(jax.ShapeDtypeStruct(tiled, BF16), ja...]
    pallas_call x1, Pallas kernels: 53.9 us -> 53.3 us  [on_device(): pl.pallas_call(functools.partial(kernel, groups, lanes, capacity), out_sh...]
where the time goes in v3:
time: 58.7 us; the launch traced here: 58.5 us
  Pallas kernels  55.2 us (94%)
  other arithmetic  2.51 us (4%)
  between operations  0.67 us (1%)
    pallas_call x1, Pallas kernels, on_device(): pl.pallas_call(functools.partial(kernel, groups, lanes, capacity), out_sh...  53.3 us
    pallas_call x1, Pallas kernels, on_device(): pl.pallas_call(hand_out, out_shape=(jax.ShapeDtypeStruct(tiled, BF16), ja...  1.88 us

profile of v3, /device:TPU:0, one launch (start us, length us, event | category | flops | bytes accessed | tf_op | source)
XLA Modules:
  0.0 58.5 jit_solution(13595276259328335121)
XLA Ops:
  0.6 0.7 %broadcast_subtract_fusion = s32[128]{0:T(128)S(1)} fusion(s32[128]{0:T(128)} %param.10, s32[]{:T(128)S(6)} %mul.21), kind=kLoop, calls=%fused_computation.20 | loop fusion | flops 128 | bytes 1028 | tf_op jit(solution)/shard_map/sub | solution.py:35
  1.3 0.7 %broadcast_compare_fusion.1 = (pred[128]{0:T(512)(128)(4,1)S(1)}, s32[128]{0:T(128)S(1)}, pred[128]{0:T(512)(128)(4,1)S(1)}) fusion(s32[]{:T(128)S(6)} %axis_index.15, s32[128]{0:T(128)} %param.10), kind=kLoop, calls=%fused_computation.23 | loop fusion | flops 1408 | bytes 1284 | tf_op jit(solution)/shard_map/eq | solution.py:43
  2.0 0.2 convert_reduce_fusion
  2.2 0.1 select_reduce_fusion.1
  2.3 0.1 dynamic_slice.3
  2.4 0.1 select_reduce_fusion.2
  2.5 0.1 select_reduce_fusion
  2.6 0.6 %pad_add_fusion.maps = s32[192]{0:T(256)} fusion(s32[96]{0:T(128)S(1)} %broadcast_add_fusion, s32[32]{0:T(128)S(1)} %select_reduce_fusion.1, s32[32]{0:T(128)S(1)} %dynamic_slice.3, s32[32]{0:T(128)S(1)} %select_reduce_fusion.2), kind=kLoop, calls=%fused_computation.12 | loop fusion | flops 576 | bytes 1536 | tf_op jit(solution)/shard_map/concatenate | solution.py:62
  3.2 53.3 %projector_norm.1 = (bf16[96,8,1024]{2,1,0:T(8,128)(2,1)S(1)}, bf16[96,8,1024]{2,1,0:T(8,128)(2,1)S(1)}, bf16[256,1024]{1,0:T(8,128)(2,1)S(1)}) custom-call(s32[192]{0:T(256)} %pad_add_fusion.maps, bf16[256,8192]{1,0:T(8,128)(2,1)} %hidden.1, bf16[8192,1024]{1,0:T(8,128)(2,1)} %weight.1, f32[1,1024]{1,0:T(1,128)} %bitcast.10, f32[1,1024]{1,0:T(1,128)} %bitcast.11, ...), custom_call_target="tpu_custom_call" | custom-call | flops 8589934592 | bytes 28835840 | tf_op jit(solution)/shard_map/projector_norm/pallas_call | solution.py:548
  56.6 1.9 %hand_out.1 = (bf16[96,8,1024]{2,1,0:T(8,128)(2,1)}, bf16[96,8,1024]{2,1,0:T(8,128)(2,1)}, bf16[256,1024]{1,0:T(8,128)(2,1)}) custom-call(bf16[96,8,1024]{2,1,0:T(8,128)(2,1)S(1)} %get-tuple-element.9.refs_0_, bf16[96,8,1024]{2,1,0:T(8,128)(2,1)S(1)} %get-tuple-element.10.refs_1_, bf16[256,1024]{1,0:T(8,128)(2,1)S(1)} %get-tuple-element.11.refs_2_), custom_call_target="tpu_custom_call" | custom-call | tf_op jit(solution)/shard_map/hand_out/pallas_call | solution.py:604
  (4 shorter events, 0.0 us)

commit v4 on v3

--- a/solution.py
+++ b/solution.py
@@ -31,8 +31,8 @@
     slots = groups * capacity
     tile_index = jnp.arange(tile_pos.shape[0], dtype=jnp.int32)
     source = tile_index // tiles_dev
-    target = lax.div(tile_pos, jnp.int32(spread))
-    local_pos = tile_pos - group_index * spread
+    local_pos = lax.optimization_barrier(tile_pos - group_index * spread)
+    target = lax.div(local_pos + group_index * spread, jnp.int32(spread))
     earlier = (
         (source[:, None] == source[None, :])
         & (target[:, None] == target[None, :])
@@ -176,14 +176,14 @@
     def _(q):
         send_dn[q] = dn_v[maps[q]]
 
-    @pl.loop(0, capacity)
-    def _(k):
-        recv_dn[grp * capacity + k] = dn_v[maps[grp * capacity + k]]
-
     pl.semaphore_wait(barrier, groups + lanes - 2)
     dn_copies = to_group(send_dn, recv_dn, dn_s, dn_r)
     for copy in dn_copies:
         copy.start()
+
+    @pl.loop(0, capacity)
+    def _(k):
+        recv_dn[grp * capacity + k] = dn_v[maps[grp * capacity + k]]
 
     gains = gain[...]
     lane = lax.broadcasted_iota(jnp.int32, (STRIP, LANES), 1)
@@ -436,11 +436,6 @@
                 flag >= 0, 0.0, d_values[side * TILE : (side + 1) * TILE, :]
             ).astype(BF16)
 
-    @pl.loop(0, rows // STRIP)
-    def _(j):
-        strip = pl.ds(pl.multiple_of(j * STRIP, STRIP), STRIP)
-        acc_v[strip, :] = gelu_slope(hid_v[tp // 2, strip, :].astype(F32))
-
     def collect(stage, last):
         for side in range(2):
             if stage >= len(plan[side]):
@@ -468,6 +463,11 @@
     stages = len(plan[0])
     for stage in range(stages - 1):
         collect(stage, False)
+
+    @pl.loop(0, rows // STRIP)
+    def _(j):
+        strip = pl.ds(pl.multiple_of(j * STRIP, STRIP), STRIP)
+        acc_v[strip, :] = gelu_slope(hid_v[tp // 2, strip, :].astype(F32))
 
     for copy in n_copies:
         copy.wait_recv()

time: 58.7 us -> 58 us (0.988)
  other arithmetic: 2.51 us -> 1.85 us
    eq x1, other arithmetic: 0.67 us -> 0.01 us  [tile_maps(): here = target == group_index]
where the time goes in v4:
time: 58 us; the launch traced here: 57.8 us
  Pallas kernels  55.1 us (95%)
  other arithmetic  1.85 us (3%)
  between operations  0.67 us (1%)
    pallas_call x1, Pallas kernels, on_device(): pl.pallas_call(functools.partial(kernel, groups, lanes, capacity), out_sh...  53.3 us
    pallas_call x1, Pallas kernels, on_device(): pl.pallas_call(hand_out, out_shape=(jax.ShapeDtypeStruct(tiled, BF16), ja...  1.88 us

profile of v4, /device:TPU:0, one launch (start us, length us, event | category | flops | bytes accessed | tf_op | source)
XLA Modules:
  0.0 57.8 jit_solution(9760900008425976067)
XLA Ops:
  0.6 0.7 %broadcast_subtract_fusion = s32[128]{0:T(128)S(1)} fusion(s32[128]{0:T(128)} %param.10, s32[]{:T(128)S(6)} %mul.21), kind=kLoop, calls=%fused_computation.24 | loop fusion | flops 128 | bytes 1028 | tf_op jit(solution)/shard_map/sub | solution.py:34
  1.3 0.2 convert_reduce_fusion
  1.5 0.1 select_reduce_fusion.1
  1.6 0.1 dynamic_slice.3
  1.7 0.1 select_reduce_fusion.2
  1.8 0.1 select_reduce_fusion
  1.9 0.6 %pad_add_fusion.maps = s32[192]{0:T(256)} fusion(s32[96]{0:T(128)S(1)} %broadcast_add_fusion, s32[32]{0:T(128)S(1)} %select_reduce_fusion.1, s32[32]{0:T(128)S(1)} %dynamic_slice.3, s32[32]{0:T(128)S(1)} %select_reduce_fusion.2), kind=kLoop, calls=%fused_computation.12 | loop fusion | flops 576 | bytes 1536 | tf_op jit(solution)/shard_map/concatenate | solution.py:62
  2.6 53.3 %projector_norm.1 = (bf16[96,8,1024]{2,1,0:T(8,128)(2,1)S(1)}, bf16[96,8,1024]{2,1,0:T(8,128)(2,1)S(1)}, bf16[256,1024]{1,0:T(8,128)(2,1)S(1)}) custom-call(s32[192]{0:T(256)} %pad_add_fusion.maps, bf16[256,8192]{1,0:T(8,128)(2,1)} %hidden.1, bf16[8192,1024]{1,0:T(8,128)(2,1)} %weight.1, f32[1,1024]{1,0:T(1,128)} %bitcast.10, f32[1,1024]{1,0:T(1,128)} %bitcast.11, ...), custom_call_target="tpu_custom_call" | custom-call | flops 8589934592 | bytes 28835840 | tf_op jit(solution)/shard_map/projector_norm/pallas_call | solution.py:548
  55.9 1.9 %hand_out.1 = (bf16[96,8,1024]{2,1,0:T(8,128)(2,1)}, bf16[96,8,1024]{2,1,0:T(8,128)(2,1)}, bf16[256,1024]{1,0:T(8,128)(2,1)}) custom-call(bf16[96,8,1024]{2,1,0:T(8,128)(2,1)S(1)} %get-tuple-element.9.refs_0_, bf16[96,8,1024]{2,1,0:T(8,128)(2,1)S(1)} %get-tuple-element.10.refs_1_, bf16[256,1024]{1,0:T(8,128)(2,1)S(1)} %get-tuple-element.11.refs_2_), custom_call_target="tpu_custom_call" | custom-call | tf_op jit(solution)/shard_map/hand_out/pallas_call | solution.py:604
  (5 shorter events, 0.0 us)
